TPU v7x, 32 devices: a whole 2x2x4 slice. The times are simulated.
32 devices in a mesh: fsdp: 16 (over z, y, x), replica: 2 (over core).
Axes of the slice: x: 2, y: 2, z: 4, core: 2. Of those that a mesh axis runs over, the one named last changes fastest.
Arguments:
- partials: float32 [2, 16384, 128], P('replica', 'fsdp'), may hold values from -6 to 6
- diag_stat: float32 [16384, 128], P('fsdp'), may hold values from 0.8 to 3
- first_stat: float32 [16384, 128], P('fsdp'), may hold values from -0.35 to 0.35
- second_stat: float32 [16384, 128], P('fsdp'), may hold values from -0.35 to 0.35
Outputs:
- update: float32 [16384, 128], P('fsdp')
- diag_next: float32 [16384, 128], P('fsdp')
- first_next: float32 [16384, 128], P('fsdp')
- second_next: float32 [16384, 128], P('fsdp')
All inputs are finite; a program needn't handle non-finite values.
Results may differ from a plain program's by a relative error of at most 0.00002.
Values sent between devices are 32-bit elements; how exact they have to be, the bound alone decides.
No kernel may reach another device: no remote copies, remote signals or barrier semaphores. Data moves between devices by JAX's collectives and lax.ppermute only.
A program may use at most 64 MiB of HBM per device.

v0:
```python
import functools

import jax
import jax.numpy as jnp
from jax import lax
from jax.experimental import pallas as pl
from jax.experimental.pallas import tpu as pltpu
from jax.sharding import PartitionSpec as P

decay_rate = 0.95
damping = 0.01
PAD = 8
TILE = 8


def solved(g, g1, g2, d, upper, lower, f, c, s):
    det = upper * lower - c * c
    n1 = lower * f - c * s
    n2 = upper * s - c * f
    schur = d * det - f * n1 - s * n2
    top = g * det - n1 * g1 - n2 * g2
    w = top / (schur * det)
    return w * det, w * n1, w * n2


def collect(rows, own, diag, first, second, far, near, tiles, sems):
    width = tiles.shape[1]
    copies = []
    for k, source in enumerate((own, diag, first, second)):
        for half, at in enumerate((0, rows - TILE)):
            row = (2 * k + half) * TILE
            copies.append(
                pltpu.make_async_copy(
                    source.at[at : at + TILE, :],
                    tiles.at[row : row + TILE, :],
                    sems.at[2 * k + half],
                )
            )
    for copy in copies:
        copy.start()
    for copy in copies:
        copy.wait()
    head = [tiles[2 * k * TILE : 2 * k * TILE + 2, :] for k in range(3)]
    head.append(jnp.ones((2, width), jnp.float32))
    last = [tiles[(2 * k + 2) * TILE - 2 : (2 * k + 2) * TILE, :] for k in range(4)]
    even = lax.rem(lax.axis_index("fsdp"), 2) == 0

    def fill(out, blocks):
        for k, block in enumerate(blocks):
            out[2 * k : 2 * k + 2, :] = block

    @pl.when(even)
    def _():
        fill(near, last)
        fill(far, head)

    @pl.when(jnp.logical_not(even))
    def _():
        fill(near, head)
        fill(far, last)


def join(far, near, out):
    out[0:2, :] = near[0:2, :]
    out[2:4, :] = far[0:2, :]
    out[4:8, :] = jnp.zeros((4, out.shape[1]), jnp.float32)


def interior(parts, scale, rows, chunk, step, *refs):
    sources = refs[0], *refs[parts : parts + 3]
    outs = refs[parts + 3 : parts + 7]
    edges = refs[parts + 7]
    staged = refs[parts + 8 : parts + 12]
    own, diag_in, first_in, second_in = staged
    pieces = [own, *refs[1:parts]]
    grad, diag, first, second, part1, part2, update, in_sems, out_sems = refs[parts + 12 :]
    width = edges.shape[1]
    end = PAD + rows
    chunks = rows // chunk

    loads = []
    for c in range(chunks):
        at = slice(c * chunk, (c + 1) * chunk)
        row = []
        for k, (source, target) in enumerate(zip(sources, staged)):
            copy = pltpu.make_async_copy(source.at[at, :], target.at[at, :], in_sems.at[k, c])
            copy.start()
            row.append(copy)
        loads.append(row)

    zeros = jnp.zeros((PAD, width), jnp.float32)
    grad[end:, :] = zeros
    diag[end:, :] = zeros + 1.0
    first[end:, :] = zeros
    part1[:PAD, :] = zeros
    part2[:PAD, :] = zeros

    def gradients(at, size):
        here, there = pl.ds(at, size), pl.ds(at + PAD, size)
        g = pieces[0][here, :]
        for piece in pieces[1:]:
            g = g + piece[here, :]
        g = g * scale
        grad[there, :] = g
        diag[there, :] = decay_rate * diag_in[here, :] + g * g

    def bands(at, size):
        here, there = pl.ds(at, size), pl.ds(at + PAD, size)
        g = grad[there, :]
        g1 = grad[pl.ds(at + PAD + 1, size), :]
        g2 = grad[pl.ds(at + PAD + 2, size), :]
        first[there, :] = decay_rate * first_in[here, :] + g * g1
        second[there, :] = decay_rate * second_in[here, :] + g * g2

    def values(at, size):
        there = pl.ds(at + PAD, size)
        after = pl.ds(at + PAD + 1, size)
        later = pl.ds(at + PAD + 2, size)
        v, p1, p2 = solved(
            grad[there, :],
            grad[after, :],
            grad[later, :],
            diag[there, :] + damping,
            diag[after, :] + damping,
            diag[later, :] + damping,
            first[there, :],
            first[after, :],
            second[there, :],
        )
        part1[there, :] = p1
        part2[there, :] = p2
        update[pl.ds(at, size), :] = (
            v - part1[pl.ds(at + PAD - 1, size), :] - part2[pl.ds(at + PAD - 2, size), :]
        )

    def over(work, low, high):
        for at in range(low, high, step):
            work(at, min(step, high - at))

    stores = []

    def send(source, pad, k, c, low, high):
        copy = pltpu.make_async_copy(
            source.at[low + pad : high + pad, :], outs[k].at[low:high, :], out_sems.at[k, c]
        )
        copy.start()
        stores.append(copy)

    for c in range(chunks):
        for copy in loads[c]:
            copy.wait()
        last = c == chunks - 1
        low, high = c * chunk, (c + 1) * chunk
        over(gradients, low, high)
        send(diag, PAD, 1, c, low, high)
        low, high = max(low - TILE, 0), high if last else high - TILE
        over(bands, low, high)
        send(first, PAD, 2, c, low, high)
        send(second, PAD, 3, c, low, high)
        low, high = max(c * chunk - 2 * TILE, 0), high if last else high - TILE
        over(values, low, high)
        send(update, 0, 0, c, low, high)

    tops = [grad[PAD : PAD + TILE, :], diag[PAD : PAD + TILE, :], first[PAD : PAD + TILE, :]]
    tops.append(update[:TILE, :])
    tails = [r[end - TILE : end, :] for r in (grad, diag, first, second)]
    tails.append(update[rows - TILE :, :])
    tails += [r[end - TILE : end, :] for r in (part1, part2)]
    for k, tile in enumerate(tops + tails):
        edges[k * TILE : (k + 1) * TILE, :] = tile
    for copy in stores:
        copy.wait()


def border(rows, shards, parts, *refs):
    edges, far, near, across = refs[:4]
    outs = refs[7:10]
    work, tiles, sems = refs[10:]

    def edge(k, at, size):
        return edges[k * TILE + at : k * TILE + at + size, :]

    shard = lax.axis_index("fsdp")
    even = lax.rem(shard, 2) == 0
    near_rows, far_rows = near[...], far[...]
    if parts > 1:
        half = 1.0 / parts
        near_rows = jnp.concatenate([(near_rows[0:2] + across[0:2, :]) * half, near_rows[2:8]])
        far_rows = jnp.concatenate([(far_rows[0:2] + across[2:4, :]) * half, far_rows[2:8]])
    before = jnp.where(even, far_rows, near_rows)
    after = jnp.where(even, near_rows, far_rows)
    work[0:8, :] = jnp.where(shard == 0, 0.0, before)
    work[8:16, :] = jnp.where(shard == shards - 1, 0.0, after)

    g = work[0:2, :]
    g_next = edge(0, 0, 2)
    d = decay_rate * work[2:4, :] + g * g + damping
    d_next = edge(1, 0, 2) + damping
    g1 = jnp.concatenate([g[1:2], g_next[0:1]])
    d1 = jnp.concatenate([d[1:2], d_next[0:1]])
    f = decay_rate * work[4:6, :] + g * g1
    s = decay_rate * work[6:8, :] + g * g_next
    c = jnp.concatenate([f[1:2], edge(2, 0, 1)])
    _, p1, p2 = solved(g, g1, g_next, d, d1, d_next, f, c, s)
    tiles[0:8, :] = edges[3 * TILE : 4 * TILE, :]
    tiles[0:1, :] = tiles[0:1, :] - p1[1:2] - p2[0:1]
    tiles[1:2, :] = tiles[1:2, :] - p2[1:2]

    g = edge(4, 6, 2)
    g_next = work[8:10, :]
    present = work[14:16, :]
    d = edge(5, 6, 2) + damping
    d_next = (
        decay_rate * work[10:12, :] + g_next * g_next + present * damping + (1.0 - present)
    )
    g1 = jnp.concatenate([g[1:2], g_next[0:1]])
    d1 = jnp.concatenate([d[1:2], d_next[0:1]])
    f_last = (edge(6, 7, 1) + g[1:2] * g_next[0:1]) * present[0:1]
    f = jnp.concatenate([edge(6, 6, 1), f_last])
    s = (edge(7, 6, 2) + g * g_next) * present
    f_next = decay_rate * work[12:13, :] + g_next[0:1] * g_next[1:2]
    c = jnp.concatenate([f_last, f_next])
    v, p1, _ = solved(g, g1, g_next, d, d1, d_next, f, c, s)
    tiles[8:16, :] = edges[8 * TILE : 9 * TILE, :]
    tiles[14:15, :] = v[0:1] - edge(9, 5, 1) - edge(10, 4, 1)
    tiles[15:16, :] = v[1:2] - p1[0:1] - edge(10, 5, 1)
    tiles[16:24, :] = edges[6 * TILE : 7 * TILE, :]
    tiles[23:24, :] = f_last
    tiles[24:32, :] = edges[7 * TILE : 8 * TILE, :]
    tiles[30:32, :] = s

    copies = [
        pltpu.make_async_copy(tiles.at[0:8, :], outs[0].at[0:TILE, :], sems.at[0]),
        pltpu.make_async_copy(tiles.at[8:16, :], outs[0].at[rows - TILE : rows, :], sems.at[1]),
        pltpu.make_async_copy(tiles.at[16:24, :], outs[1].at[rows - TILE : rows, :], sems.at[2]),
        pltpu.make_async_copy(tiles.at[24:32, :], outs[2].at[rows - TILE : rows, :], sems.at[3]),
    ]
    for copy in copies:
        copy.start()
    for copy in copies:
        copy.wait()


def matching(shards, low):
    turn = []
    partner = {}
    for i in range(low, shards - 1, 2):
        partner[i], partner[i + 1] = i + 1, i
    for i in range(shards):
        for core in range(2):
            target = (partner[i], core) if i in partner else (i, 1 - core)
            turn.append((2 * i + core, 2 * target[0] + target[1]))
    return turn


def body(partials, diag_stat, first_stat, second_stat):
    own = partials[0]
    rows, width = own.shape
    replicas = lax.axis_size("replica")
    shards = lax.axis_size("fsdp")
    scale = 1.0 / replicas
    shard = lax.axis_index("fsdp")
    axes = ("fsdp", "replica")
    paired = replicas == 2

    shape = jax.ShapeDtypeStruct((rows, width), jnp.float32)
    vmem = pl.BlockSpec(memory_space=pltpu.VMEM)
    hbm = pl.BlockSpec(memory_space=pl.ANY)
    params = pltpu.CompilerParams(vmem_limit_bytes=24 * 2**20)

    def swap(block):
        return lax.ppermute(block, "replica", [(0, 1), (1, 0)])

    def stay(block):
        return pltpu.with_memory_space_constraint(block, pltpu.HBM)

    stats = (diag_stat, first_stat, second_stat)
    held = [stay(x) for x in (own, *stats)]
    small = pltpu.VMEM((TILE, width), jnp.float32)
    if paired:
        far, near = pl.pallas_call(
            functools.partial(collect, rows),
            out_shape=(small,) * 2,
            in_specs=[hbm] * 4,
            out_specs=(vmem,) * 2,
            scratch_shapes=[
                pltpu.VMEM((8 * TILE, width), jnp.float32),
                pltpu.SemaphoreType.DMA((8,)),
            ],
            compiler_params=params,
            name="collect",
        )(*held)
        pieces = [own, swap(own)]
        far = lax.ppermute(far, axes, matching(shards, 1))
        near = lax.ppermute(near, axes, matching(shards, 0))
    else:
        pieces = [lax.psum(own, "replica") * scale]
        scale = 1.0
        tail = rows - 2
        ones = jnp.ones((2, width), jnp.float32)
        last = jnp.concatenate([x[tail:] for x in (*pieces, *stats)])
        head = jnp.concatenate([x[:2] for x in (*pieces, *stats[:2])] + [ones])
        even = shard % 2 == 0
        before = lax.ppermute(last, "fsdp", [(i, i + 1) for i in range(shards - 1)])
        after = lax.ppermute(head, "fsdp", [(i + 1, i) for i in range(shards - 1)])
        near, far = jnp.where(even, after, before), jnp.where(even, before, after)

    parts = len(pieces)
    pieces_in = [held[0], *pieces[1:]] if paired else [stay(pieces[0])]
    whole = pltpu.VMEM((rows, width), jnp.float32)
    padded = pltpu.VMEM((rows + 2 * PAD, width), jnp.float32)
    chunk = 256 if rows % 256 == 0 else rows
    update, diag_next, first_next, second_next, edges = pl.pallas_call(
        functools.partial(interior, parts, scale, rows, chunk, 64),
        out_shape=(shape,) * 4 + (pltpu.VMEM((11 * TILE, width), jnp.float32),),
        in_specs=[hbm] + [vmem] * (parts - 1) + [hbm] * 3,
        out_specs=(hbm,) * 4 + (vmem,),
        scratch_shapes=[whole] * 4
        + [padded] * 6
        + [whole]
        + [pltpu.SemaphoreType.DMA((4, rows // chunk))] * 2,
        compiler_params=params,
        cost_estimate=pl.CostEstimate(
            flops=45 * rows * width, bytes_accessed=36 * rows * width, transcendentals=0
        ),
        name="interior",
    )(*pieces_in, *held[1:])

    far, near, edges = lax.optimization_barrier((far, near, edges))
    across = near
    if paired:
        across = swap(
            pl.pallas_call(
                join,
                out_shape=small,
                in_specs=[vmem] * 2,
                out_specs=vmem,
                compiler_params=params,
                name="join",
            )(far, near)
        )

    update, first_next, second_next = pl.pallas_call(
        functools.partial(border, rows, shards, parts),
        out_shape=(shape,) * 3,
        in_specs=[vmem] * 4 + [hbm] * 3,
        out_specs=(hbm,) * 3,
        input_output_aliases={4: 0, 5: 1, 6: 2},
        scratch_shapes=[
            pltpu.VMEM((16, width), jnp.float32),
            pltpu.VMEM((32, width), jnp.float32),
            pltpu.SemaphoreType.DMA((4,)),
        ],
        compiler_params=params,
        name="border",
    )(edges, far, near, across, update, first_next, second_next)
    return update, diag_next, first_next, second_next


def solution(mesh):
    return jax.shard_map(
        body,
        mesh=mesh,
        in_specs=(P("replica", "fsdp", None), P("fsdp", None), P("fsdp", None), P("fsdp", None)),
        out_specs=(P("fsdp", None), P("fsdp", None), P("fsdp", None), P("fsdp", None)),
        check_vma=False,
    )
```

profile of v0, /device:TPU:0, one launch (start us, length us, event | category | flops | bytes accessed | tf_op | source)
XLA Modules:
  0.0 11.0 jit_solution(5553689240199729709)
XLA Ops:
  0.6 0.5 %collective-permute-start.2 = (f32[1024,128]{1,0:T(8,128)}, f32[1024,128]{1,0:T(8,128)S(1)}, u32[]{:S(2)}, u32[]{:S(2)}) collective-permute-start(f32[1024,128]{1,0:T(8,128)} %bitcast.1), channel_id=1, source_target_pairs={{0,1},{1,0},{2,3},{3,2},{4,5},{5,4},{6,7},{7,6},{8,9},{9,8},{10,11... | collective-permute-start | bytes 1572872 | tf_op jit(solution)/shard_map/ppermute | solution.py:272
  1.1 0.9 %collect.1 = (f32[8,128]{1,0:T(8,128)S(1)}, f32[8,128]{1,0:T(8,128)S(1)}) custom-call(f32[1024,128]{1,0:T(8,128)} %bitcast.2, f32[1024,128]{1,0:T(8,128)} %refs_2_.1, f32[1024,128]{1,0:T(8,128)} %refs_3_.1, f32[1024,128]{1,0:T(8,128)} %refs_4_.1), custom_call_target="tpu_custom_call" | custom-call | tf_op jit(solution)/shard_map/collect/pallas_call | solution.py:281
  2.0 0.1 %collective-permute-start = (f32[8,128]{1,0:T(8,128)S(1)}, f32[8,128]{1,0:T(8,128)S(1)}, u32[]{:S(2)}, u32[]{:S(2)}) collective-permute-start(f32[8,128]{1,0:T(8,128)S(1)} %get-tuple-element.17), channel_id=1, source_target_pairs={{0,1},{1,0},{2,4},{3,5},{4,2},{5,3},{6,8},{7,9},{8,6},{9,7},{10,12... | collective-permute-start | bytes 12296 | tf_op jit(solution)/shard_map/ppermute | solution.py:294
  2.2 3.9 %collective-permute-start.1 = (f32[8,128]{1,0:T(8,128)S(1)}, f32[8,128]{1,0:T(8,128)S(1)}, u32[]{:S(2)}, u32[]{:S(2)}) collective-permute-start(f32[8,128]{1,0:T(8,128)S(1)} %get-tuple-element.18), channel_id=1, source_target_pairs={{0,2},{1,3},{2,0},{3,1},{4,6},{5,7},{6,4},{7,5},{8,10},{9,11},{10,... | collective-permute-start | bytes 12296 | tf_op jit(solution)/shard_map/ppermute | solution.py:295
  6.1 0.0 collective-permute-done.2.refs_1_
  6.1 3.0 %interior.1 = (f32[1024,128]{1,0:T(8,128)}, f32[1024,128]{1,0:T(8,128)}, f32[1024,128]{1,0:T(8,128)}, f32[1024,128]{1,0:T(8,128)}, f32[88,128]{1,0:T(8,128)S(1)}) custom-call(f32[1024,128]{1,0:T(8,128)} %bitcast.3, f32[1024,128]{1,0:T(8,128)S(1)} %collective-permute-done.2.refs_1_, f32[1024,128]{1,0:T(8,128)} %refs_2_.1, f32[1024,128]{1,0:T(8,128)} %refs_3_.1, ...), custom_call_target="tpu_custom_call" | custom-call | flops 5898240 | bytes 4718592 | tf_op jit(solution)/shard_map/interior/pallas_call | solution.py:313
  9.1 0.0 collective-permute-done.far.refs_1_
  9.1 0.0 collective-permute-done.1.near.refs_2_
  9.1 0.1 collective-permute-start.3
  9.2 1.2 %collective-permute-done.3.refs_3_ = f32[8,128]{1,0:T(8,128)S(1)} collective-permute-done((f32[8,128]{1,0:T(8,128)S(1)}, f32[8,128]{1,0:T(8,128)S(1)}, u32[]{:S(2)}, u32[]{:S(2)}) %collective-permute-start.3) | collective-permute-done | bytes 4128 | tf_op jit(solution)/shard_map/ppermute | solution.py:272
  10.3 0.7 %border.1 = (f32[1024,128]{1,0:T(8,128)}, f32[1024,128]{1,0:T(8,128)}, f32[1024,128]{1,0:T(8,128)}) custom-call(f32[88,128]{1,0:T(8,128)S(1)} %get-tuple-element.20.refs_0_, f32[8,128]{1,0:T(8,128)S(1)} %collective-permute-done.far.refs_1_, ...), custom_call_target="tpu_custom_call", output_to_operand_aliasing={{0}: (4, {}), {1}: (5, {}), {2}: (6, {})} | custom-call | tf_op jit(solution)/shard_map/border/pallas_call | solution.py:343
  (1 shorter events, 0.0 us)
Async XLA Ops:
  0.6 5.5 %collective-permute-start.2 = (f32[1024,128]{1,0:T(8,128)}, f32[1024,128]{1,0:T(8,128)S(1)}, u32[]{:S(2)}, u32[]{:S(2)}) collective-permute-start(f32[1024,128]{1,0:T(8,128)} %bitcast.1), channel_id=1, source_target_pairs={{0,1},{1,0},{2,3},{3,2},{4,5},{5,4},{6,7},{7,6},{8,9},{9,8},{10,11... | collective-permute-start | bytes 1572872 | tf_op jit(solution)/shard_map/ppermute | solution.py:272
  2.0 7.0 %collective-permute-start = (f32[8,128]{1,0:T(8,128)S(1)}, f32[8,128]{1,0:T(8,128)S(1)}, u32[]{:S(2)}, u32[]{:S(2)}) collective-permute-start(f32[8,128]{1,0:T(8,128)S(1)} %get-tuple-element.17), channel_id=1, source_target_pairs={{0,1},{1,0},{2,4},{3,5},{4,2},{5,3},{6,8},{7,9},{8,6},{9,7},{10,12... | collective-permute-start | bytes 12296 | tf_op jit(solution)/shard_map/ppermute | solution.py:294
  2.2 6.9 %collective-permute-start.1 = (f32[8,128]{1,0:T(8,128)S(1)}, f32[8,128]{1,0:T(8,128)S(1)}, u32[]{:S(2)}, u32[]{:S(2)}) collective-permute-start(f32[8,128]{1,0:T(8,128)S(1)} %get-tuple-element.18), channel_id=1, source_target_pairs={{0,2},{1,3},{2,0},{3,1},{4,6},{5,7},{6,4},{7,5},{8,10},{9,11},{10,... | collective-permute-start | bytes 12296 | tf_op jit(solution)/shard_map/ppermute | solution.py:295
  9.1 1.2 %collective-permute-start.3 = (f32[8,128]{1,0:T(8,128)S(1)}, f32[8,128]{1,0:T(8,128)S(1)}, u32[]{:S(2)}, u32[]{:S(2)}) collective-permute-start(f32[8,128]{1,0:T(8,128)S(1)} %join.1), channel_id=1, source_target_pairs={{0,1},{1,0},{2,3},{3,2},{4,5},{5,4},{6,7},{7,6},{8,9},{9,8},{10,11... | collective-permute-start | bytes 12296 | tf_op jit(solution)/shard_map/ppermute | solution.py:272
where the time goes:
time: 11.2 us; the launch traced here: 11 us
  starting transfers between devices  4.65 us (42%)
  Pallas kernels  4.51 us (40%)
  waiting for transfers between devices  1.16 us (10%)
  between operations  0.68 us (6%)
    ppermute x1, starting transfers between devices, body(): near = lax.ppermute(near, axes, matching(shards, 0))  3.94 us
    pallas_call x1, Pallas kernels, body(): pl.pallas_call(functools.partial(interior, parts, scale, rows, chunk, 64)...  2.95 us
    ppermute x2, waiting for transfers between devices, swap(): return lax.ppermute(block, 'replica', [(0, 1), (1, 0)])  1.16 us
    pallas_call x1, Pallas kernels, body(): pl.pallas_call(functools.partial(collect, rows), out_shape=(small,) * 2,...  0.87 us
    pallas_call x1, Pallas kernels, body(): pl.pallas_call(functools.partial(border, rows, shards, parts), out_shape=...  0.68 us
    ppermute x2, starting transfers between devices, swap(): return lax.ppermute(block, 'replica', [(0, 1), (1, 0)])  0.59 us
  transfers between devices with their start and end apart: 4, of which 1 were waited for; matrix products, arithmetic and copies ran while one was open for 0% of the time, Pallas kernels for 35%

commit v1 on v0

--- a/solution.py
+++ b/solution.py
@@ -67,26 +67,14 @@
 
 
 def interior(parts, scale, rows, chunk, step, *refs):
-    sources = refs[0], *refs[parts : parts + 3]
+    pieces = refs[:parts]
+    diag_in, first_in, second_in = refs[parts : parts + 3]
     outs = refs[parts + 3 : parts + 7]
     edges = refs[parts + 7]
-    staged = refs[parts + 8 : parts + 12]
-    own, diag_in, first_in, second_in = staged
-    pieces = [own, *refs[1:parts]]
-    grad, diag, first, second, part1, part2, update, in_sems, out_sems = refs[parts + 12 :]
+    grad, diag, first, second, part1, part2, update, sems = refs[parts + 8 :]
     width = edges.shape[1]
     end = PAD + rows
     chunks = rows // chunk
-
-    loads = []
-    for c in range(chunks):
-        at = slice(c * chunk, (c + 1) * chunk)
-        row = []
-        for k, (source, target) in enumerate(zip(sources, staged)):
-            copy = pltpu.make_async_copy(source.at[at, :], target.at[at, :], in_sems.at[k, c])
-            copy.start()
-            row.append(copy)
-        loads.append(row)
 
     zeros = jnp.zeros((PAD, width), jnp.float32)
     grad[end:, :] = zeros
@@ -141,14 +129,12 @@
 
     def send(source, pad, k, c, low, high):
         copy = pltpu.make_async_copy(
-            source.at[low + pad : high + pad, :], outs[k].at[low:high, :], out_sems.at[k, c]
+            source.at[low + pad : high + pad, :], outs[k].at[low:high, :], sems.at[k, c]
         )
         copy.start()
         stores.append(copy)
 
     for c in range(chunks):
-        for copy in loads[c]:
-            copy.wait()
         last = c == chunks - 1
         low, high = c * chunk, (c + 1) * chunk
         over(gradients, low, high)
@@ -306,25 +292,21 @@
         near, far = jnp.where(even, after, before), jnp.where(even, before, after)
 
     parts = len(pieces)
-    pieces_in = [held[0], *pieces[1:]] if paired else [stay(pieces[0])]
     whole = pltpu.VMEM((rows, width), jnp.float32)
     padded = pltpu.VMEM((rows + 2 * PAD, width), jnp.float32)
     chunk = 256 if rows % 256 == 0 else rows
     update, diag_next, first_next, second_next, edges = pl.pallas_call(
         functools.partial(interior, parts, scale, rows, chunk, 64),
         out_shape=(shape,) * 4 + (pltpu.VMEM((11 * TILE, width), jnp.float32),),
-        in_specs=[hbm] + [vmem] * (parts - 1) + [hbm] * 3,
+        in_specs=[vmem] * (parts + 3),
         out_specs=(hbm,) * 4 + (vmem,),
-        scratch_shapes=[whole] * 4
-        + [padded] * 6
-        + [whole]
-        + [pltpu.SemaphoreType.DMA((4, rows // chunk))] * 2,
+        scratch_shapes=[padded] * 6 + [whole, pltpu.SemaphoreType.DMA((4, rows // chunk))],
         compiler_params=params,
         cost_estimate=pl.CostEstimate(
             flops=45 * rows * width, bytes_accessed=36 * rows * width, transcendentals=0
         ),
         name="interior",
-    )(*pieces_in, *held[1:])
+    )(*[pltpu.with_memory_space_constraint(x, pltpu.VMEM) for x in (*pieces, *stats)])
 
     far, near, edges = lax.optimization_barrier((far, near, edges))
     across = near

time: 11.2 us -> 10.1 us (0.902)
  the two profiles are of different devices: /device:TPU:0 before, /device:TPU:9 now
where the time goes in v1:
time: 10.1 us; the launch traced here: 9.91 us
  starting transfers between devices  4.47 us (44%)
  Pallas kernels  3.24 us (32%)
  waiting for transfers between devices  1.48 us (15%)
  between operations  0.7 us (7%)
    ppermute x1, starting transfers between devices, body(): far = lax.ppermute(far, axes, matching(shards, 1))  2.14 us
    ppermute x2, starting transfers between devices, swap(): return lax.ppermute(block, 'replica', [(0, 1), (1, 0)])  1.96 us
    pallas_call x1, Pallas kernels, body(): pl.pallas_call(functools.partial(interior, parts, scale, rows, chunk, 64)...  1.69 us
    pallas_call x1, Pallas kernels, body(): pl.pallas_call(functools.partial(collect, rows), out_shape=(small,) * 2,...  0.87 us
    ppermute x2, waiting for transfers between devices, swap(): return lax.ppermute(block, 'replica', [(0, 1), (1, 0)])  0.83 us
    pallas_call x1, Pallas kernels, body(): pl.pallas_call(functools.partial(border, rows, shards, parts), out_shape=...  0.68 us
    ppermute x1, waiting for transfers between devices, body(): near = lax.ppermute(near, axes, matching(shards, 0))  0.55 us
    ppermute x1, starting transfers between devices, body(): near = lax.ppermute(near, axes, matching(shards, 0))  0.37 us
  transfers between devices with their start and end apart: 4, of which 3 were waited for; matrix products, arithmetic and copies ran while one was open for 0% of the time, Pallas kernels for 26%

profile of v1, /device:TPU:9, one launch (start us, length us, event | category | flops | bytes accessed | tf_op | source)
XLA Modules:
  0.0 9.9 jit_solution(9970805369205974240)
XLA Ops:
  0.6 0.0 copy-start
  0.6 0.0 copy-start.1
  0.7 0.0 copy-start.2
  0.7 0.0 copy-start.3
  0.7 0.7 %collective-permute-start.2 = (f32[1024,128]{1,0:T(8,128)}, f32[1024,128]{1,0:T(8,128)S(1)}, u32[]{:S(2)}, u32[]{:S(2)}) collective-permute-start(f32[1024,128]{1,0:T(8,128)} %bitcast.1), channel_id=1, source_target_pairs={{0,1},{1,0},{2,3},{3,2},{4,5},{5,4},{6,7},{7,6},{8,9},{9,8},{10,11... | collective-permute-start | bytes 1572872 | tf_op jit(solution)/shard_map/ppermute | solution.py:258
  1.4 0.9 %collect.1 = (f32[8,128]{1,0:T(8,128)S(1)}, f32[8,128]{1,0:T(8,128)S(1)}) custom-call(f32[1024,128]{1,0:T(8,128)} %bitcast.2, f32[1024,128]{1,0:T(8,128)} %refs_2_.1, f32[1024,128]{1,0:T(8,128)} %refs_3_.1, f32[1024,128]{1,0:T(8,128)} %refs_4_.1), custom_call_target="tpu_custom_call" | custom-call | tf_op jit(solution)/shard_map/collect/pallas_call | solution.py:267
  2.3 2.1 %collective-permute-start = (f32[8,128]{1,0:T(8,128)S(1)}, f32[8,128]{1,0:T(8,128)S(1)}, u32[]{:S(2)}, u32[]{:S(2)}) collective-permute-start(f32[8,128]{1,0:T(8,128)S(1)} %get-tuple-element.17), channel_id=1, source_target_pairs={{0,1},{1,0},{2,4},{3,5},{4,2},{5,3},{6,8},{7,9},{8,6},{9,7},{10,12... | collective-permute-start | bytes 12296 | tf_op jit(solution)/shard_map/ppermute | solution.py:280
  4.4 0.4 %collective-permute-start.1 = (f32[8,128]{1,0:T(8,128)S(1)}, f32[8,128]{1,0:T(8,128)S(1)}, u32[]{:S(2)}, u32[]{:S(2)}) collective-permute-start(f32[8,128]{1,0:T(8,128)S(1)} %get-tuple-element.18), channel_id=1, source_target_pairs={{0,2},{1,3},{2,0},{3,1},{4,6},{5,7},{6,4},{7,5},{8,10},{9,11},{10,... | collective-permute-start | bytes 12296 | tf_op jit(solution)/shard_map/ppermute | solution.py:281
  4.8 0.0 collective-permute-done.2.refs_1_
  4.8 0.0 copy-done
  4.8 0.0 copy-done.1
  4.8 0.0 copy-done.2
  4.8 0.0 copy-done.3
  4.8 1.7 %interior.1 = (f32[1024,128]{1,0:T(8,128)}, f32[1024,128]{1,0:T(8,128)}, f32[1024,128]{1,0:T(8,128)}, f32[1024,128]{1,0:T(8,128)}, f32[88,128]{1,0:T(8,128)S(1)}) custom-call(f32[1024,128]{1,0:T(8,128)S(1)} %bitcast.3, f32[1024,128]{1,0:T(8,128)S(1)} %collective-permute-done.2.refs_1_, f32[1024,128]{1,0:T(8,128)S(1)} %copy-done.1, ...), custom_call_target="tpu_custom_call" | custom-call | flops 5898240 | bytes 4718592 | tf_op jit(solution)/shard_map/interior/pallas_call | solution.py:298
  6.5 0.1 %collective-permute-done.far.refs_1_ = f32[8,128]{1,0:T(8,128)S(1)} collective-permute-done((f32[8,128]{1,0:T(8,128)S(1)}, f32[8,128]{1,0:T(8,128)S(1)}, u32[]{:S(2)}, u32[]{:S(2)}) %collective-permute-start) | collective-permute-done | bytes 4128 | tf_op jit(solution)/shard_map/ppermute | solution.py:280
  6.6 0.5 %collective-permute-done.1.near.refs_2_ = f32[8,128]{1,0:T(8,128)S(1)} collective-permute-done((f32[8,128]{1,0:T(8,128)S(1)}, f32[8,128]{1,0:T(8,128)S(1)}, u32[]{:S(2)}, u32[]{:S(2)}) %collective-permute-start.1) | collective-permute-done | bytes 4128 | tf_op jit(solution)/shard_map/ppermute | solution.py:281
  7.2 1.2 %collective-permute-start.3 = (f32[8,128]{1,0:T(8,128)S(1)}, f32[8,128]{1,0:T(8,128)S(1)}, u32[]{:S(2)}, u32[]{:S(2)}) collective-permute-start(f32[8,128]{1,0:T(8,128)S(1)} %join.1), channel_id=1, source_target_pairs={{0,1},{1,0},{2,3},{3,2},{4,5},{5,4},{6,7},{7,6},{8,9},{9,8},{10,11... | collective-permute-start | bytes 12296 | tf_op jit(solution)/shard_map/ppermute | solution.py:258
  8.4 0.8 %collective-permute-done.3.refs_3_ = f32[8,128]{1,0:T(8,128)S(1)} collective-permute-done((f32[8,128]{1,0:T(8,128)S(1)}, f32[8,128]{1,0:T(8,128)S(1)}, u32[]{:S(2)}, u32[]{:S(2)}) %collective-permute-start.3) | collective-permute-done | bytes 4128 | tf_op jit(solution)/shard_map/ppermute | solution.py:258
  9.2 0.7 %border.1 = (f32[1024,128]{1,0:T(8,128)}, f32[1024,128]{1,0:T(8,128)}, f32[1024,128]{1,0:T(8,128)}) custom-call(f32[88,128]{1,0:T(8,128)S(1)} %get-tuple-element.20.refs_0_, f32[8,128]{1,0:T(8,128)S(1)} %collective-permute-done.far.refs_1_, ...), custom_call_target="tpu_custom_call", output_to_operand_aliasing={{0}: (4, {}), {1}: (5, {}), {2}: (6, {})} | custom-call | tf_op jit(solution)/shard_map/border/pallas_call | solution.py:325
  (1 shorter events, 0.0 us)
Async XLA Ops:
  0.6 4.2 %copy-start = (f32[1,1024,128]{2,1,0:T(8,128)S(1)}, f32[1,1024,128]{2,1,0:T(8,128)}, u32[]{:S(2)}) copy-start(f32[1,1024,128]{2,1,0:T(8,128)} %param.4) | copy-start | bytes 1572868
  0.6 4.2 %copy-start.1 = (f32[1024,128]{1,0:T(8,128)S(1)}, f32[1024,128]{1,0:T(8,128)}, u32[]{:S(2)}) copy-start(f32[1024,128]{1,0:T(8,128)} %refs_2_.1) | copy-start | bytes 1572868
  0.7 4.2 %copy-start.2 = (f32[1024,128]{1,0:T(8,128)S(1)}, f32[1024,128]{1,0:T(8,128)}, u32[]{:S(2)}) copy-start(f32[1024,128]{1,0:T(8,128)} %refs_3_.1) | copy-start | bytes 1572868
  0.7 4.2 %copy-start.3 = (f32[1024,128]{1,0:T(8,128)S(1)}, f32[1024,128]{1,0:T(8,128)}, u32[]{:S(2)}) copy-start(f32[1024,128]{1,0:T(8,128)} %refs_4_.1) | copy-start | bytes 1572868
  0.7 4.1 %collective-permute-start.2 = (f32[1024,128]{1,0:T(8,128)}, f32[1024,128]{1,0:T(8,128)S(1)}, u32[]{:S(2)}, u32[]{:S(2)}) collective-permute-start(f32[1024,128]{1,0:T(8,128)} %bitcast.1), channel_id=1, source_target_pairs={{0,1},{1,0},{2,3},{3,2},{4,5},{5,4},{6,7},{7,6},{8,9},{9,8},{10,11... | collective-permute-start | bytes 1572872 | tf_op jit(solution)/shard_map/ppermute | solution.py:258
  2.3 4.3 %collective-permute-start = (f32[8,128]{1,0:T(8,128)S(1)}, f32[8,128]{1,0:T(8,128)S(1)}, u32[]{:S(2)}, u32[]{:S(2)}) collective-permute-start(f32[8,128]{1,0:T(8,128)S(1)} %get-tuple-element.17), channel_id=1, source_target_pairs={{0,1},{1,0},{2,4},{3,5},{4,2},{5,3},{6,8},{7,9},{8,6},{9,7},{10,12... | collective-permute-start | bytes 12296 | tf_op jit(solution)/shard_map/ppermute | solution.py:280
  4.4 2.8 %collective-permute-start.1 = (f32[8,128]{1,0:T(8,128)S(1)}, f32[8,128]{1,0:T(8,128)S(1)}, u32[]{:S(2)}, u32[]{:S(2)}) collective-permute-start(f32[8,128]{1,0:T(8,128)S(1)} %get-tuple-element.18), channel_id=1, source_target_pairs={{0,2},{1,3},{2,0},{3,1},{4,6},{5,7},{6,4},{7,5},{8,10},{9,11},{10,... | collective-permute-start | bytes 12296 | tf_op jit(solution)/shard_map/ppermute | solution.py:281
  7.2 2.0 %collective-permute-start.3 = (f32[8,128]{1,0:T(8,128)S(1)}, f32[8,128]{1,0:T(8,128)S(1)}, u32[]{:S(2)}, u32[]{:S(2)}) collective-permute-start(f32[8,128]{1,0:T(8,128)S(1)} %join.1), channel_id=1, source_target_pairs={{0,1},{1,0},{2,3},{3,2},{4,5},{5,4},{6,7},{7,6},{8,9},{9,8},{10,11... | collective-permute-start | bytes 12296 | tf_op jit(solution)/shard_map/ppermute | solution.py:258

commit v2 on v1

--- a/solution.py
+++ b/solution.py
@@ -21,6 +21,11 @@
     top = g * det - n1 * g1 - n2 * g2
     w = top / (schur * det)
     return w * det, w * n1, w * n2
+
+
+def over(work, low, high, step):
+    for at in range(low, high, step):
+        work(at, min(step, high - at))
 
 
 def collect(rows, own, diag, first, second, far, near, tiles, sems):
@@ -60,28 +65,32 @@
         fill(far, last)
 
 
-def join(far, near, out):
-    out[0:2, :] = near[0:2, :]
-    out[2:4, :] = far[0:2, :]
-    out[4:8, :] = jnp.zeros((4, out.shape[1]), jnp.float32)
-
-
-def interior(parts, scale, rows, chunk, step, *refs):
+def ready(scale, rows, near, other, out):
+    even = lax.rem(lax.axis_index("fsdp"), 2) == 0
+    out[2:8, :] = near[2:8, :]
+
+    @pl.when(even)
+    def _():
+        out[0:2, :] = (near[0:2, :] + other[rows - 2 : rows, :]) * scale
+
+    @pl.when(jnp.logical_not(even))
+    def _():
+        out[0:2, :] = (near[0:2, :] + other[0:2, :]) * scale
+
+
+def bands(parts, scale, rows, chunk, step, *refs):
     pieces = refs[:parts]
     diag_in, first_in, second_in = refs[parts : parts + 3]
-    outs = refs[parts + 3 : parts + 7]
-    edges = refs[parts + 7]
-    grad, diag, first, second, part1, part2, update, sems = refs[parts + 8 :]
-    width = edges.shape[1]
+    outs = refs[parts + 3 : parts + 6]
+    grad, diag, first, second, sems = refs[parts + 6 :]
+    width = diag_in.shape[1]
     end = PAD + rows
     chunks = rows // chunk
 
     zeros = jnp.zeros((PAD, width), jnp.float32)
-    grad[end:, :] = zeros
-    diag[end:, :] = zeros + 1.0
-    first[end:, :] = zeros
-    part1[:PAD, :] = zeros
-    part2[:PAD, :] = zeros
+    for padded, edge in ((grad, zeros), (diag, zeros + 1.0), (first, zeros), (second, zeros)):
+        padded[:PAD, :] = edge
+        padded[end:, :] = edge
 
     def gradients(at, size):
         here, there = pl.ds(at, size), pl.ds(at + PAD, size)
@@ -92,13 +101,42 @@
         grad[there, :] = g
         diag[there, :] = decay_rate * diag_in[here, :] + g * g
 
-    def bands(at, size):
+    def products(at, size):
         here, there = pl.ds(at, size), pl.ds(at + PAD, size)
         g = grad[there, :]
         g1 = grad[pl.ds(at + PAD + 1, size), :]
         g2 = grad[pl.ds(at + PAD + 2, size), :]
         first[there, :] = decay_rate * first_in[here, :] + g * g1
         second[there, :] = decay_rate * second_in[here, :] + g * g2
+
+    stores = []
+
+    def send(source, k, c, low, high):
+        copy = pltpu.make_async_copy(
+            source.at[low + PAD : high + PAD, :], outs[k].at[low:high, :], sems.at[k, c]
+        )
+        copy.start()
+        stores.append(copy)
+
+    for c in range(chunks):
+        low, high = c * chunk, (c + 1) * chunk
+        over(gradients, low, high, step)
+        send(diag, 0, c, low, high)
+        low, high = max(low - TILE, 0), high if c == chunks - 1 else high - TILE
+        over(products, low, high, step)
+        send(first, 1, c, low, high)
+        send(second, 2, c, low, high)
+    for copy in stores:
+        copy.wait()
+
+
+def updates(rows, chunk, step, *refs):
+    grad, diag, first, second, out, edges, part1, part2, update, sems = refs
+    width = grad.shape[1]
+    end = PAD + rows
+    zeros = jnp.zeros((PAD, width), jnp.float32)
+    part1[:PAD, :] = zeros
+    part2[:PAD, :] = zeros
 
     def values(at, size):
         there = pl.ds(at + PAD, size)
@@ -121,31 +159,13 @@
             v - part1[pl.ds(at + PAD - 1, size), :] - part2[pl.ds(at + PAD - 2, size), :]
         )
 
-    def over(work, low, high):
-        for at in range(low, high, step):
-            work(at, min(step, high - at))
-
     stores = []
-
-    def send(source, pad, k, c, low, high):
-        copy = pltpu.make_async_copy(
-            source.at[low + pad : high + pad, :], outs[k].at[low:high, :], sems.at[k, c]
-        )
+    for c in range(rows // chunk):
+        low, high = c * chunk, (c + 1) * chunk
+        over(values, low, high, step)
+        copy = pltpu.make_async_copy(update.at[low:high, :], out.at[low:high, :], sems.at[c])
         copy.start()
         stores.append(copy)
-
-    for c in range(chunks):
-        last = c == chunks - 1
-        low, high = c * chunk, (c + 1) * chunk
-        over(gradients, low, high)
-        send(diag, PAD, 1, c, low, high)
-        low, high = max(low - TILE, 0), high if last else high - TILE
-        over(bands, low, high)
-        send(first, PAD, 2, c, low, high)
-        send(second, PAD, 3, c, low, high)
-        low, high = max(c * chunk - 2 * TILE, 0), high if last else high - TILE
-        over(values, low, high)
-        send(update, 0, 0, c, low, high)
 
     tops = [grad[PAD : PAD + TILE, :], diag[PAD : PAD + TILE, :], first[PAD : PAD + TILE, :]]
     tops.append(update[:TILE, :])
@@ -170,9 +190,8 @@
     even = lax.rem(shard, 2) == 0
     near_rows, far_rows = near[...], far[...]
     if parts > 1:
-        half = 1.0 / parts
-        near_rows = jnp.concatenate([(near_rows[0:2] + across[0:2, :]) * half, near_rows[2:8]])
-        far_rows = jnp.concatenate([(far_rows[0:2] + across[2:4, :]) * half, far_rows[2:8]])
+        far_sum = (far_rows[0:2] + across[0:2, :]) * (1.0 / parts)
+        far_rows = jnp.concatenate([far_sum, far_rows[2:8]])
     before = jnp.where(even, far_rows, near_rows)
     after = jnp.where(even, near_rows, far_rows)
     work[0:8, :] = jnp.where(shard == 0, 0.0, before)
@@ -278,6 +297,14 @@
         )(*held)
         pieces = [own, swap(own)]
         far = lax.ppermute(far, axes, matching(shards, 1))
+        near = pl.pallas_call(
+            functools.partial(ready, scale, rows),
+            out_shape=small,
+            in_specs=[vmem] * 2,
+            out_specs=vmem,
+            compiler_params=params,
+            name="ready",
+        )(near, pieces[1])
         near = lax.ppermute(near, axes, matching(shards, 0))
     else:
         pieces = [lax.psum(own, "replica") * scale]
@@ -295,32 +322,29 @@
     whole = pltpu.VMEM((rows, width), jnp.float32)
     padded = pltpu.VMEM((rows + 2 * PAD, width), jnp.float32)
     chunk = 256 if rows % 256 == 0 else rows
-    update, diag_next, first_next, second_next, edges = pl.pallas_call(
-        functools.partial(interior, parts, scale, rows, chunk, 64),
-        out_shape=(shape,) * 4 + (pltpu.VMEM((11 * TILE, width), jnp.float32),),
+    cost = 20 * rows * width
+    diag_next, first_next, second_next, *work = pl.pallas_call(
+        functools.partial(bands, parts, scale, rows, chunk, 64),
+        out_shape=(shape,) * 3 + (padded,) * 4,
         in_specs=[vmem] * (parts + 3),
-        out_specs=(hbm,) * 4 + (vmem,),
-        scratch_shapes=[padded] * 6 + [whole, pltpu.SemaphoreType.DMA((4, rows // chunk))],
+        out_specs=(hbm,) * 3 + (vmem,) * 4,
+        scratch_shapes=[pltpu.SemaphoreType.DMA((3, rows // chunk))],
         compiler_params=params,
-        cost_estimate=pl.CostEstimate(
-            flops=45 * rows * width, bytes_accessed=36 * rows * width, transcendentals=0
-        ),
-        name="interior",
+        cost_estimate=pl.CostEstimate(flops=cost, bytes_accessed=cost, transcendentals=0),
+        name="bands",
     )(*[pltpu.with_memory_space_constraint(x, pltpu.VMEM) for x in (*pieces, *stats)])
-
-    far, near, edges = lax.optimization_barrier((far, near, edges))
-    across = near
-    if paired:
-        across = swap(
-            pl.pallas_call(
-                join,
-                out_shape=small,
-                in_specs=[vmem] * 2,
-                out_specs=vmem,
-                compiler_params=params,
-                name="join",
-            )(far, near)
-        )
+    far, work[0] = lax.optimization_barrier((far, work[0]))
+    across = swap(far) if paired else far
+    update, edges = pl.pallas_call(
+        functools.partial(updates, rows, chunk, 64),
+        out_shape=(shape, pltpu.VMEM((11 * TILE, width), jnp.float32)),
+        in_specs=[vmem] * 4,
+        out_specs=(hbm, vmem),
+        scratch_shapes=[padded] * 2 + [whole, pltpu.SemaphoreType.DMA((rows // chunk,))],
+        compiler_params=params,
+        cost_estimate=pl.CostEstimate(flops=cost, bytes_accessed=cost, transcendentals=0),
+        name="updates",
+    )(*[pltpu.with_memory_space_constraint(x, pltpu.VMEM) for x in work])
 
     update, first_next, second_next = pl.pallas_call(
         functools.partial(border, rows, shards, parts),

time: 10.1 us -> 10.2 us (level)
  Pallas kernels: 3.24 us -> 4.3 us
  waiting for transfers between devices: 1.48 us -> 0.49 us
    pallas_call x2 -> x3, Pallas kernels: 1.69 us -> 2.64 us  [the longest x1 1.37 us: body(): pl.pallas_call(functools.partial(updates, rows, chunk, 64), out_shape=(sh...]
    ppermute x2, waiting for transfers between devices: 0.83 us -> 0.01 us  [swap(): return lax.ppermute(block, 'replica', [(0, 1), (1, 0)])]
    ppermute x1, waiting for transfers between devices: 0.55 us -> 0.01 us  [body(): near = lax.ppermute(near, axes, matching(shards, 0))]
    ppermute x1, waiting for transfers between devices: 0.11 us -> 0.48 us  [body(): far = lax.ppermute(far, axes, matching(shards, 1))]
  transfers between devices with their start and end apart: 4 -> 4, of which waited for: 3 -> 1; matrix products, arithmetic and copies ran while one was open for 0% -> 0% of each run, Pallas kernels for 26% -> 36%
where the time goes in v2:
time: 10.2 us; the launch traced here: 9.97 us
  starting transfers between devices  4.48 us (44%)
  Pallas kernels  4.3 us (42%)
  between operations  0.69 us (7%)
  waiting for transfers between devices  0.49 us (5%)
    ppermute x1, starting transfers between devices, body(): far = lax.ppermute(far, axes, matching(shards, 1))  2.12 us
    ppermute x2, starting transfers between devices, swap(): return lax.ppermute(block, 'replica', [(0, 1), (1, 0)])  1.93 us
    pallas_call x1, Pallas kernels, body(): pl.pallas_call(functools.partial(updates, rows, chunk, 64), out_shape=(sh...  1.37 us
    pallas_call x1, Pallas kernels, body(): pl.pallas_call(functools.partial(bands, parts, scale, rows, chunk, 64), o...  1.27 us
    pallas_call x1, Pallas kernels, body(): pl.pallas_call(functools.partial(collect, rows), out_shape=(small,) * 2,...  0.97 us
    pallas_call x1, Pallas kernels, body(): pl.pallas_call(functools.partial(border, rows, shards, parts), out_shape=...  0.69 us
    ppermute x1, waiting for transfers between devices, body(): far = lax.ppermute(far, axes, matching(shards, 1))  0.48 us
    ppermute x1, starting transfers between devices, body(): near = lax.ppermute(near, axes, matching(shards, 0))  0.43 us
  transfers between devices with their start and end apart: 4, of which 1 were waited for; matrix products, arithmetic and copies ran while one was open for 0% of the time, Pallas kernels for 36%

profile of v2, /device:TPU:9, one launch (start us, length us, event | category | flops | bytes accessed | tf_op | source)
XLA Modules:
  0.0 10.0 jit_solution(16873517246717574276)
XLA Ops:
  0.6 0.7 %collective-permute-start.1 = (f32[1024,128]{1,0:T(8,128)}, f32[1024,128]{1,0:T(8,128)S(1)}, u32[]{:S(2)}, u32[]{:S(2)}) collective-permute-start(f32[1024,128]{1,0:T(8,128)} %bitcast.1), channel_id=1, source_target_pairs={{0,1},{1,0},{2,3},{3,2},{4,5},{5,4},{6,7},{7,6},{8,9},{9,8},{10,11... | collective-permute-start | bytes 1572872 | tf_op jit(solution)/shard_map/ppermute | solution.py:277
  1.4 0.0 copy-start.1
  1.4 0.0 copy-start.2
  1.4 0.0 copy-start.3
  1.4 1.0 %collect.1 = (f32[8,128]{1,0:T(8,128)S(1)}, f32[8,128]{1,0:T(8,128)S(1)}) custom-call(f32[1024,128]{1,0:T(8,128)} %bitcast.2, f32[1024,128]{1,0:T(8,128)} %refs_2_.1, f32[1024,128]{1,0:T(8,128)} %refs_3_.1, f32[1024,128]{1,0:T(8,128)} %refs_4_.1), custom_call_target="tpu_custom_call" | custom-call | tf_op jit(solution)/shard_map/collect/pallas_call | solution.py:286
  2.4 0.0 copy-start
  2.4 2.1 %collective-permute-start = (f32[8,128]{1,0:T(8,128)S(1)}, f32[8,128]{1,0:T(8,128)S(1)}, u32[]{:S(2)}, u32[]{:S(2)}) collective-permute-start(f32[8,128]{1,0:T(8,128)S(1)} %get-tuple-element.20), channel_id=1, source_target_pairs={{0,1},{1,0},{2,4},{3,5},{4,2},{5,3},{6,8},{7,9},{8,6},{9,7},{10,12... | collective-permute-start | bytes 12296 | tf_op jit(solution)/shard_map/ppermute | solution.py:299
  4.5 0.0 collective-permute-done.1.refs_1_.other
  4.5 0.4 %collective-permute-start.2 = (f32[8,128]{1,0:T(8,128)S(1)}, f32[8,128]{1,0:T(8,128)S(1)}, u32[]{:S(2)}, u32[]{:S(2)}) collective-permute-start(f32[8,128]{1,0:T(8,128)S(1)} %ready.1), channel_id=1, source_target_pairs={{0,2},{1,3},{2,0},{3,1},{4,6},{5,7},{6,4},{7,5},{8,10},{9,11},{10,... | collective-permute-start | bytes 12296 | tf_op jit(solution)/shard_map/ppermute | solution.py:308
  4.9 0.0 copy-done.1
  4.9 0.0 copy-done.2
  4.9 0.0 copy-done.3
  4.9 0.0 copy-done
  4.9 1.3 %bands.1 = (f32[1024,128]{1,0:T(8,128)}, f32[1024,128]{1,0:T(8,128)}, f32[1024,128]{1,0:T(8,128)}, f32[1040,128]{1,0:T(8,128)S(1)}, f32[1040,128]{1,0:T(8,128)S(...) custom-call(f32[1024,128]{1,0:T(8,128)S(1)} %bitcast.3, f32[1024,128]{1,0:T(8,128)S(1)} %collective-permute-done.1.refs_1_.other, ...), custom_call_target="tpu_custom_call" | custom-call | flops 2621440 | bytes 2621440 | tf_op jit(solution)/shard_map/bands/pallas_call | solution.py:326
  6.2 0.5 %collective-permute-done.refs_1_ = f32[8,128]{1,0:T(8,128)S(1)} collective-permute-done((f32[8,128]{1,0:T(8,128)S(1)}, f32[8,128]{1,0:T(8,128)S(1)}, u32[]{:S(2)}, u32[]{:S(2)}) %collective-permute-start) | collective-permute-done | bytes 4128 | tf_op jit(solution)/shard_map/ppermute | solution.py:299
  6.7 1.2 %collective-permute-start.3 = (f32[8,128]{1,0:T(8,128)S(1)}, f32[8,128]{1,0:T(8,128)S(1)}, u32[]{:S(2)}, u32[]{:S(2)}) collective-permute-start(f32[8,128]{1,0:T(8,128)S(1)} %collective-permute-done.refs_1_), channel_id=1, source_target_pairs={{0,1},{1,0},{2,3},{3,2},{4,5},{5,4},{6,7},{7,6},{8,9},{9,8},{10,11... | collective-permute-start | bytes 12296 | tf_op jit(solution)/shard_map/ppermute | solution.py:277
  7.9 1.4 %updates.1 = (f32[1024,128]{1,0:T(8,128)}, f32[88,128]{1,0:T(8,128)S(1)}) custom-call(f32[1040,128]{1,0:T(8,128)S(1)} %get-tuple-element.22.refs_0_, f32[1040,128]{1,0:T(8,128)S(1)} %get-tuple-element.23.refs_1_, f32[1040,128]{1,0:T(8,128)S(1)} %get-tuple-element.24.refs_2_, f32[1040,128]{1,0:T(8,128)S(1)} %get-tuple-element.25.refs_3_), custom_call_target="tpu_custom_call" | custom-call | flops 2621440 | bytes 2621440 | tf_op jit(solution)/shard_map/updates/pallas_call | solution.py:338
  9.3 0.0 collective-permute-done.2.refs_2_
  9.3 0.0 collective-permute-done.3.refs_3_
  9.3 0.7 %border.1 = (f32[1024,128]{1,0:T(8,128)}, f32[1024,128]{1,0:T(8,128)}, f32[1024,128]{1,0:T(8,128)}) custom-call(f32[88,128]{1,0:T(8,128)S(1)} %get-tuple-element.26.refs_0_, f32[8,128]{1,0:T(8,128)S(1)} %collective-permute-done.refs_1_, f32[8,128]{1,0:T(8,128)S(1)} %collective-permute-done.2.refs_2_, ...), custom_call_target="tpu_custom_call", output_to_operand_aliasing={{0}: (4, {}), {1}: (5, {}), {2}: (6, {})} | custom-call | tf_op jit(solution)/shard_map/border/pallas_call | solution.py:349
  (1 shorter events, 0.0 us)
Async XLA Ops:
  0.6 3.9 %collective-permute-start.1 = (f32[1024,128]{1,0:T(8,128)}, f32[1024,128]{1,0:T(8,128)S(1)}, u32[]{:S(2)}, u32[]{:S(2)}) collective-permute-start(f32[1024,128]{1,0:T(8,128)} %bitcast.1), channel_id=1, source_target_pairs={{0,1},{1,0},{2,3},{3,2},{4,5},{5,4},{6,7},{7,6},{8,9},{9,8},{10,11... | collective-permute-start | bytes 1572872 | tf_op jit(solution)/shard_map/ppermute | solution.py:277
  1.4 3.6 %copy-start.1 = (f32[1024,128]{1,0:T(8,128)S(1)}, f32[1024,128]{1,0:T(8,128)}, u32[]{:S(2)}) copy-start(f32[1024,128]{1,0:T(8,128)} %refs_2_.1) | copy-start | bytes 1572868
  1.4 3.6 %copy-start.2 = (f32[1024,128]{1,0:T(8,128)S(1)}, f32[1024,128]{1,0:T(8,128)}, u32[]{:S(2)}) copy-start(f32[1024,128]{1,0:T(8,128)} %refs_3_.1) | copy-start | bytes 1572868
  1.4 3.6 %copy-start.3 = (f32[1024,128]{1,0:T(8,128)S(1)}, f32[1024,128]{1,0:T(8,128)}, u32[]{:S(2)}) copy-start(f32[1024,128]{1,0:T(8,128)} %refs_4_.1) | copy-start | bytes 1572868
  2.4 2.6 %copy-start = (f32[1,1024,128]{2,1,0:T(8,128)S(1)}, f32[1,1024,128]{2,1,0:T(8,128)}, u32[]{:S(2)}) copy-start(f32[1,1024,128]{2,1,0:T(8,128)} %param.4) | copy-start | bytes 1572868
  2.4 4.3 %collective-permute-start = (f32[8,128]{1,0:T(8,128)S(1)}, f32[8,128]{1,0:T(8,128)S(1)}, u32[]{:S(2)}, u32[]{:S(2)}) collective-permute-start(f32[8,128]{1,0:T(8,128)S(1)} %get-tuple-element.20), channel_id=1, source_target_pairs={{0,1},{1,0},{2,4},{3,5},{4,2},{5,3},{6,8},{7,9},{8,6},{9,7},{10,12... | collective-permute-start | bytes 12296 | tf_op jit(solution)/shard_map/ppermute | solution.py:299
  4.5 4.8 %collective-permute-start.2 = (f32[8,128]{1,0:T(8,128)S(1)}, f32[8,128]{1,0:T(8,128)S(1)}, u32[]{:S(2)}, u32[]{:S(2)}) collective-permute-start(f32[8,128]{1,0:T(8,128)S(1)} %ready.1), channel_id=1, source_target_pairs={{0,2},{1,3},{2,0},{3,1},{4,6},{5,7},{6,4},{7,5},{8,10},{9,11},{10,... | collective-permute-start | bytes 12296 | tf_op jit(solution)/shard_map/ppermute | solution.py:308
  6.7 2.6 %collective-permute-start.3 = (f32[8,128]{1,0:T(8,128)S(1)}, f32[8,128]{1,0:T(8,128)S(1)}, u32[]{:S(2)}, u32[]{:S(2)}) collective-permute-start(f32[8,128]{1,0:T(8,128)S(1)} %collective-permute-done.refs_1_), channel_id=1, source_target_pairs={{0,1},{1,0},{2,3},{3,2},{4,5},{5,4},{6,7},{7,6},{8,9},{9,8},{10,11... | collective-permute-start | bytes 12296 | tf_op jit(solution)/shard_map/ppermute | solution.py:277

commit v3 on v1

--- a/solution.py
+++ b/solution.py
@@ -60,18 +60,38 @@
         fill(far, last)
 
 
-def join(far, near, out):
-    out[0:2, :] = near[0:2, :]
-    out[2:4, :] = far[0:2, :]
-    out[4:8, :] = jnp.zeros((4, out.shape[1]), jnp.float32)
-
-
-def interior(parts, scale, rows, chunk, step, *refs):
-    pieces = refs[:parts]
-    diag_in, first_in, second_in = refs[parts : parts + 3]
-    outs = refs[parts + 3 : parts + 7]
-    edges = refs[parts + 7]
-    grad, diag, first, second, part1, part2, update, sems = refs[parts + 8 :]
+def ready(scale, rows, far, near, other, far_out, near_out):
+    even = lax.rem(lax.axis_index("fsdp"), 2) == 0
+    for out, block in ((far_out, far), (near_out, near)):
+        out[2:8, :] = block[2:8, :]
+
+    def fill(out, block, at):
+        out[0:2, :] = (block[0:2, :] + other[at : at + 2, :]) * scale
+
+    @pl.when(even)
+    def _():
+        fill(far_out, far, 0)
+        fill(near_out, near, rows - 2)
+
+    @pl.when(jnp.logical_not(even))
+    def _():
+        fill(far_out, far, rows - 2)
+        fill(near_out, near, 0)
+
+
+def interior(parts, early, scale, rows, chunk, step, *refs):
+    chosen = lax.axis_index("fsdp") == 0
+
+    @pl.when(chosen if early else jnp.logical_not(chosen))
+    def _():
+        everything(parts, scale, rows, chunk, step, refs[: parts + 3], refs[-13:])
+
+
+def everything(parts, scale, rows, chunk, step, ins, rest):
+    pieces = ins[:parts]
+    diag_in, first_in, second_in = ins[parts:]
+    outs, edges = rest[:4], rest[4]
+    grad, diag, first, second, part1, part2, update, sems = rest[5:]
     width = edges.shape[1]
     end = PAD + rows
     chunks = rows // chunk
@@ -158,21 +178,17 @@
         copy.wait()
 
 
-def border(rows, shards, parts, *refs):
-    edges, far, near, across = refs[:4]
-    outs = refs[7:10]
-    work, tiles, sems = refs[10:]
+def border(rows, shards, *refs):
+    edges, far, near = refs[:3]
+    outs = refs[6:9]
+    work, tiles, sems = refs[9:]
 
     def edge(k, at, size):
         return edges[k * TILE + at : k * TILE + at + size, :]
 
     shard = lax.axis_index("fsdp")
     even = lax.rem(shard, 2) == 0
-    near_rows, far_rows = near[...], far[...]
-    if parts > 1:
-        half = 1.0 / parts
-        near_rows = jnp.concatenate([(near_rows[0:2] + across[0:2, :]) * half, near_rows[2:8]])
-        far_rows = jnp.concatenate([(far_rows[0:2] + across[2:4, :]) * half, far_rows[2:8]])
+    far_rows, near_rows = far[...], near[...]
     before = jnp.where(even, far_rows, near_rows)
     after = jnp.where(even, near_rows, far_rows)
     work[0:8, :] = jnp.where(shard == 0, 0.0, before)
@@ -227,15 +243,15 @@
         copy.wait()
 
 
-def matching(shards, low):
-    turn = []
+def matching(shards, replicas, low):
     partner = {}
     for i in range(low, shards - 1, 2):
         partner[i], partner[i + 1] = i + 1, i
+    turn = []
     for i in range(shards):
-        for core in range(2):
-            target = (partner[i], core) if i in partner else (i, 1 - core)
-            turn.append((2 * i + core, 2 * target[0] + target[1]))
+        for r in range(replicas):
+            target = (partner[i], r) if i in partner else (i, r ^ 1)
+            turn.append((replicas * i + r, replicas * target[0] + target[1]))
     return turn
 
 
@@ -277,8 +293,14 @@
             name="collect",
         )(*held)
         pieces = [own, swap(own)]
-        far = lax.ppermute(far, axes, matching(shards, 1))
-        near = lax.ppermute(near, axes, matching(shards, 0))
+        far, near = pl.pallas_call(
+            functools.partial(ready, scale, rows),
+            out_shape=(small,) * 2,
+            in_specs=[vmem] * 3,
+            out_specs=(vmem,) * 2,
+            compiler_params=params,
+            name="ready",
+        )(far, near, pieces[1])
     else:
         pieces = [lax.psum(own, "replica") * scale]
         scale = 1.0
@@ -287,47 +309,42 @@
         last = jnp.concatenate([x[tail:] for x in (*pieces, *stats)])
         head = jnp.concatenate([x[:2] for x in (*pieces, *stats[:2])] + [ones])
         even = shard % 2 == 0
-        before = lax.ppermute(last, "fsdp", [(i, i + 1) for i in range(shards - 1)])
-        after = lax.ppermute(head, "fsdp", [(i + 1, i) for i in range(shards - 1)])
-        near, far = jnp.where(even, after, before), jnp.where(even, before, after)
+        far, near = jnp.where(even, head, last), jnp.where(even, last, head)
 
     parts = len(pieces)
     whole = pltpu.VMEM((rows, width), jnp.float32)
     padded = pltpu.VMEM((rows + 2 * PAD, width), jnp.float32)
     chunk = 256 if rows % 256 == 0 else rows
-    update, diag_next, first_next, second_next, edges = pl.pallas_call(
-        functools.partial(interior, parts, scale, rows, chunk, 64),
-        out_shape=(shape,) * 4 + (pltpu.VMEM((11 * TILE, width), jnp.float32),),
-        in_specs=[vmem] * (parts + 3),
-        out_specs=(hbm,) * 4 + (vmem,),
-        scratch_shapes=[padded] * 6 + [whole, pltpu.SemaphoreType.DMA((4, rows // chunk))],
-        compiler_params=params,
-        cost_estimate=pl.CostEstimate(
-            flops=45 * rows * width, bytes_accessed=36 * rows * width, transcendentals=0
-        ),
-        name="interior",
-    )(*[pltpu.with_memory_space_constraint(x, pltpu.VMEM) for x in (*pieces, *stats)])
-
-    far, near, edges = lax.optimization_barrier((far, near, edges))
-    across = near
-    if paired:
-        across = swap(
-            pl.pallas_call(
-                join,
-                out_shape=small,
-                in_specs=[vmem] * 2,
-                out_specs=vmem,
-                compiler_params=params,
-                name="join",
-            )(far, near)
-        )
+    inner = [pltpu.with_memory_space_constraint(x, pltpu.VMEM) for x in (*pieces, *stats)]
+    edge_shape = pltpu.VMEM((11 * TILE, width), jnp.float32)
+
+    def inside(early, *done):
+        return pl.pallas_call(
+            functools.partial(interior, parts, early, scale, rows, chunk, 64),
+            out_shape=(shape,) * 4 + (edge_shape,),
+            in_specs=[vmem] * (parts + 3) + ([hbm] * 4 + [vmem] if done else []),
+            out_specs=(hbm,) * 4 + (vmem,),
+            input_output_aliases={parts + 3 + k: k for k in range(len(done))},
+            scratch_shapes=[padded] * 6 + [whole, pltpu.SemaphoreType.DMA((4, rows // chunk))],
+            compiler_params=params,
+            cost_estimate=pl.CostEstimate(
+                flops=45 * rows * width, bytes_accessed=36 * rows * width, transcendentals=0
+            ),
+            name="early" if early else "late",
+        )(*inner, *done)
+
+    far = lax.ppermute(far, axes, matching(shards, replicas, 1))
+    done = inside(True)
+    near, *done = lax.optimization_barrier((near, *done))
+    near = lax.ppermute(near, axes, matching(shards, replicas, 0))
+    update, diag_next, first_next, second_next, edges = inside(False, *done)
 
     update, first_next, second_next = pl.pallas_call(
-        functools.partial(border, rows, shards, parts),
+        functools.partial(border, rows, shards),
         out_shape=(shape,) * 3,
-        in_specs=[vmem] * 4 + [hbm] * 3,
+        in_specs=[vmem] * 3 + [hbm] * 3,
         out_specs=(hbm,) * 3,
-        input_output_aliases={4: 0, 5: 1, 6: 2},
+        input_output_aliases={3: 0, 4: 1, 5: 2},
         scratch_shapes=[
             pltpu.VMEM((16, width), jnp.float32),
             pltpu.VMEM((32, width), jnp.float32),
@@ -335,7 +352,7 @@
         ],
         compiler_params=params,
         name="border",
-    )(edges, far, near, across, update, first_next, second_next)
+    )(edges, far, near, update, first_next, second_next)
     return update, diag_next, first_next, second_next
 
 

time: 10.1 us -> 9.96 us (0.986)
  the two profiles are of different devices: /device:TPU:9 before, /device:TPU:0 now
where the time goes in v3:
time: 9.96 us; the launch traced here: 9.77 us
  Pallas kernels  3.49 us (35%)
  starting transfers between devices  3.4 us (34%)
  waiting for transfers between devices  2.18 us (22%)
  between operations  0.68 us (7%)
    ppermute x1, starting transfers between devices, body(): near = lax.ppermute(near, axes, matching(shards, replicas, 0))  2.51 us
    pallas_call x2, Pallas kernels, inside(): pl.pallas_call(functools.partial(interior, parts, early, scale, rows, chu...  1.84 us
    ppermute x1, waiting for transfers between devices, body(): near = lax.ppermute(near, axes, matching(shards, replicas, 0))  1.43 us
    pallas_call x1, Pallas kernels, body(): pl.pallas_call(functools.partial(collect, rows), out_shape=(small,) * 2,...  0.97 us
    ppermute x1, waiting for transfers between devices, swap(): return lax.ppermute(block, 'replica', [(0, 1), (1, 0)])  0.76 us
    pallas_call x1, Pallas kernels, body(): pl.pallas_call(functools.partial(border, rows, shards), out_shape=(shape,...  0.68 us
    ppermute x1, starting transfers between devices, swap(): return lax.ppermute(block, 'replica', [(0, 1), (1, 0)])  0.52 us
    ppermute x1, starting transfers between devices, body(): far = lax.ppermute(far, axes, matching(shards, replicas, 1))  0.37 us
  transfers between devices with their start and end apart: 3, of which 2 were waited for; matrix products, arithmetic and copies ran while one was open for 0% of the time, Pallas kernels for 29%

profile of v3, /device:TPU:0, one launch (start us, length us, event | category | flops | bytes accessed | tf_op | source)
XLA Modules:
  0.0 9.8 jit_solution(16707342888004033256)
XLA Ops:
  0.6 0.5 %collective-permute-start = (f32[1024,128]{1,0:T(8,128)}, f32[1024,128]{1,0:T(8,128)S(1)}, u32[]{:S(2)}, u32[]{:S(2)}) collective-permute-start(f32[1024,128]{1,0:T(8,128)} %bitcast.1), channel_id=1, source_target_pairs={{0,1},{1,0},{2,3},{3,2},{4,5},{5,4},{6,7},{7,6},{8,9},{9,8},{10,11... | collective-permute-start | bytes 1572872 | tf_op jit(solution)/shard_map/ppermute | solution.py:274
  1.1 0.0 copy-start.1
  1.2 0.0 copy-start.2
  1.2 0.0 copy-start.3
  1.2 1.0 %collect.1 = (f32[8,128]{1,0:T(8,128)S(1)}, f32[8,128]{1,0:T(8,128)S(1)}) custom-call(f32[1024,128]{1,0:T(8,128)} %bitcast.2, f32[1024,128]{1,0:T(8,128)} %refs_2_.3, f32[1024,128]{1,0:T(8,128)} %refs_3_.3, f32[1024,128]{1,0:T(8,128)} %refs_4_.3), custom_call_target="tpu_custom_call" | custom-call | tf_op jit(solution)/shard_map/collect/pallas_call | solution.py:283
  2.1 0.0 copy-start
  2.1 0.8 %collective-permute-done.other.refs_1_ = f32[1024,128]{1,0:T(8,128)S(1)} collective-permute-done((f32[1024,128]{1,0:T(8,128)}, f32[1024,128]{1,0:T(8,128)S(1)}, u32[]{:S(2)}, u32[]{:S(2)}) %collective-permute-start) | collective-permute-done | bytes 524320 | tf_op jit(solution)/shard_map/ppermute | solution.py:274
  2.9 0.4 %collective-permute-start.1 = (f32[8,128]{1,0:T(8,128)S(1)}, f32[8,128]{1,0:T(8,128)S(1)}, u32[]{:S(2)}, u32[]{:S(2)}) collective-permute-start(f32[8,128]{1,0:T(8,128)S(1)} %get-tuple-element.41), channel_id=1, source_target_pairs={{0,1},{1,0},{2,4},{3,5},{4,2},{5,3},{6,8},{7,9},{8,6},{9,7},{10,12... | collective-permute-start | bytes 12296 | tf_op jit(solution)/shard_map/ppermute | solution.py:336
  3.3 0.0 copy-done.1
  3.3 0.0 copy-done.2
  3.3 0.0 copy-done.3
  3.3 0.0 copy-done
  3.3 1.7 %early.1 = (f32[1024,128]{1,0:T(8,128)}, f32[1024,128]{1,0:T(8,128)}, f32[1024,128]{1,0:T(8,128)}, f32[1024,128]{1,0:T(8,128)}, f32[88,128]{1,0:T(8,128)S(1)}) custom-call(f32[1024,128]{1,0:T(8,128)S(1)} %bitcast.3, f32[1024,128]{1,0:T(8,128)S(1)} %collective-permute-done.other.refs_1_, f32[1024,128]{1,0:T(8,128)S(1)} %copy-done.1, ...), custom_call_target="tpu_custom_call" | custom-call | flops 5898240 | bytes 4718592 | tf_op jit(solution)/shard_map/early/pallas_call | solution.py:322
  5.0 2.5 %collective-permute-start.2 = (f32[8,128]{1,0:T(8,128)S(1)}, f32[8,128]{1,0:T(8,128)S(1)}, u32[]{:S(2)}, u32[]{:S(2)}) collective-permute-start(f32[8,128]{1,0:T(8,128)S(1)} %get-tuple-element.42), channel_id=1, source_target_pairs={{0,2},{1,3},{2,0},{3,1},{4,6},{5,7},{6,4},{7,5},{8,10},{9,11},{10,... | collective-permute-start | bytes 12296 | tf_op jit(solution)/shard_map/ppermute | solution.py:339
  7.5 0.1 %late.1 = (f32[1024,128]{1,0:T(8,128)}, f32[1024,128]{1,0:T(8,128)}, f32[1024,128]{1,0:T(8,128)}, f32[1024,128]{1,0:T(8,128)}, f32[88,128]{1,0:T(8,128)S(1)}) custom-call(f32[1024,128]{1,0:T(8,128)S(1)} %bitcast.4, ...), custom_call_target="tpu_custom_call", output_to_operand_aliasing={{0}: (5, {}), {1}: (6, {}), {2}: (7, {}), {3}: (8, {}), {4}... | custom-call | flops 5898240 | bytes 4718592 | tf_op jit(solution)/shard_map/late/pallas_call | solution.py:322
  7.7 0.0 collective-permute-done.1.refs_1_
  7.7 1.4 %collective-permute-done.2.refs_2_ = f32[8,128]{1,0:T(8,128)S(1)} collective-permute-done((f32[8,128]{1,0:T(8,128)S(1)}, f32[8,128]{1,0:T(8,128)S(1)}, u32[]{:S(2)}, u32[]{:S(2)}) %collective-permute-start.2) | collective-permute-done | bytes 4128 | tf_op jit(solution)/shard_map/ppermute | solution.py:339
  9.1 0.7 %border.1 = (f32[1024,128]{1,0:T(8,128)}, f32[1024,128]{1,0:T(8,128)}, f32[1024,128]{1,0:T(8,128)}) custom-call(f32[88,128]{1,0:T(8,128)S(1)} %get-tuple-element.40.refs_0_, f32[8,128]{1,0:T(8,128)S(1)} %collective-permute-done.1.refs_1_, f32[8,128]{1,0:T(8,128)S(1)} %collective-permute-done.2.refs_2_, ...), custom_call_target="tpu_custom_call", output_to_operand_aliasing={{0}: (3, {}), {1}: (4, {}), {2}: (5, {})} | custom-call | tf_op jit(solution)/shard_map/border/pallas_call | solution.py:342
  (1 shorter events, 0.0 us)
Async XLA Ops:
  0.6 2.3 %collective-permute-start = (f32[1024,128]{1,0:T(8,128)}, f32[1024,128]{1,0:T(8,128)S(1)}, u32[]{:S(2)}, u32[]{:S(2)}) collective-permute-start(f32[1024,128]{1,0:T(8,128)} %bitcast.1), channel_id=1, source_target_pairs={{0,1},{1,0},{2,3},{3,2},{4,5},{5,4},{6,7},{7,6},{8,9},{9,8},{10,11... | collective-permute-start | bytes 1572872 | tf_op jit(solution)/shard_map/ppermute | solution.py:274
  1.1 2.1 %copy-start.1 = (f32[1024,128]{1,0:T(8,128)S(1)}, f32[1024,128]{1,0:T(8,128)}, u32[]{:S(2)}) copy-start(f32[1024,128]{1,0:T(8,128)} %refs_2_.3) | copy-start | bytes 1572868
  1.2 2.1 %copy-start.2 = (f32[1024,128]{1,0:T(8,128)S(1)}, f32[1024,128]{1,0:T(8,128)}, u32[]{:S(2)}) copy-start(f32[1024,128]{1,0:T(8,128)} %refs_3_.3) | copy-start | bytes 1572868
  1.2 2.1 %copy-start.3 = (f32[1024,128]{1,0:T(8,128)S(1)}, f32[1024,128]{1,0:T(8,128)}, u32[]{:S(2)}) copy-start(f32[1024,128]{1,0:T(8,128)} %refs_4_.3) | copy-start | bytes 1572868
  2.1 1.2 %copy-start = (f32[1,1024,128]{2,1,0:T(8,128)S(1)}, f32[1,1024,128]{2,1,0:T(8,128)}, u32[]{:S(2)}) copy-start(f32[1,1024,128]{2,1,0:T(8,128)} %param.4) | copy-start | bytes 1572868
  2.9 4.8 %collective-permute-start.1 = (f32[8,128]{1,0:T(8,128)S(1)}, f32[8,128]{1,0:T(8,128)S(1)}, u32[]{:S(2)}, u32[]{:S(2)}) collective-permute-start(f32[8,128]{1,0:T(8,128)S(1)} %get-tuple-element.41), channel_id=1, source_target_pairs={{0,1},{1,0},{2,4},{3,5},{4,2},{5,3},{6,8},{7,9},{8,6},{9,7},{10,12... | collective-permute-start | bytes 12296 | tf_op jit(solution)/shard_map/ppermute | solution.py:336
  5.0 4.1 %collective-permute-start.2 = (f32[8,128]{1,0:T(8,128)S(1)}, f32[8,128]{1,0:T(8,128)S(1)}, u32[]{:S(2)}, u32[]{:S(2)}) collective-permute-start(f32[8,128]{1,0:T(8,128)S(1)} %get-tuple-element.42), channel_id=1, source_target_pairs={{0,2},{1,3},{2,0},{3,1},{4,6},{5,7},{6,4},{7,5},{8,10},{9,11},{10,... | collective-permute-start | bytes 12296 | tf_op jit(solution)/shard_map/ppermute | solution.py:339
